TPU v7x, 32 devices: a whole 2x2x4 slice. The times are simulated.
32 devices in a mesh: fsdp: 32 (over z, y, x, core).
Axes of the slice: x: 2, y: 2, z: 4, core: 2. Of those that a mesh axis runs over, the one named last changes fastest.
Arguments:
- tokens: bfloat16 [32768, 768], P('fsdp'), may hold values from -6 to 6
- encoder_states: bfloat16 [32768, 768], P('fsdp'), may hold values from -6 to 6
- self_query: bfloat16 [589824], P('fsdp'), may hold values from -0.109375 to 0.109375
- self_key: bfloat16 [589824], P('fsdp'), may hold values from -0.109375 to 0.109375
- self_value: bfloat16 [589824], P('fsdp'), may hold values from -0.21875 to 0.21875
- self_out: bfloat16 [589824], P('fsdp'), may hold values from -0.875 to 0.875
- cross_query: bfloat16 [589824], P('fsdp'), may hold values from -0.109375 to 0.109375
- cross_key: bfloat16 [589824], P('fsdp'), may hold values from -0.109375 to 0.109375
- cross_value: bfloat16 [589824], P('fsdp'), may hold values from -0.21875 to 0.21875
- cross_out: bfloat16 [589824], P('fsdp'), may hold values from -0.875 to 0.875
- ff_gate: bfloat16 [1572864], P('fsdp'), may hold values from -0.21875 to 0.21875
- ff_up: bfloat16 [1572864], P('fsdp'), may hold values from -0.21875 to 0.21875
- ff_down: bfloat16 [1572864], P('fsdp'), may hold values from -0.25 to 0.25
- norm_gains: bfloat16 [3, 768], replicated, may hold values from 0.5 to 1.5
- bias_table: bfloat16 [32, 12], replicated, may hold values from -4 to 4
- buckets: int32 [512, 512], replicated, may hold values from 0 to 31, as said below
- cotangent: bfloat16 [32768, 768], P('fsdp'), may hold values from -6 to 6
Outputs:
- output: bfloat16 [32768, 768], P('fsdp')
- tokens_grad: bfloat16 [32768, 768], P('fsdp')
- encoder_grad: bfloat16 [32768, 768], P('fsdp')
- grad_self_query: float32 [589824], P('fsdp')
- grad_self_key: float32 [589824], P('fsdp')
- grad_self_value: float32 [589824], P('fsdp')
- grad_self_out: float32 [589824], P('fsdp')
- grad_cross_query: float32 [589824], P('fsdp')
- grad_cross_key: float32 [589824], P('fsdp')
- grad_cross_value: float32 [589824], P('fsdp')
- grad_cross_out: float32 [589824], P('fsdp')
- grad_ff_gate: float32 [1572864], P('fsdp')
- grad_ff_up: float32 [1572864], P('fsdp')
- grad_ff_down: float32 [1572864], P('fsdp')
- gains_grad: float32 [3, 768], replicated
- table_grad: float32 [32, 12], replicated
Inputs may be any that keep to these rules, and one draw needn't show every extreme that they name: buckets[i, j] depends only on i - j; it is 0 where j > i, equals i - j where i - j < 16, does not fall as i - j grows and is 31 at the largest distances.
All inputs are finite; a program needn't handle non-finite values.
Results may differ from a plain program's by a relative error of at most 0.025.
The roundings to bfloat16 on the way count: a program that leaves them out, or rounds other values in their place, can miss the bound.
Values may be sent and summed in bfloat16 or wider, within the bound.
No kernel may reach another device: no remote copies, remote signals or barrier semaphores. Data moves between devices by JAX's collectives and lax.ppermute only.
A program may use at most 256 MiB of HBM per device.

v0:
```python
from functools import partial

import jax
import jax.numpy as jnp
from jax import lax
from jax.sharding import PartitionSpec as P

D = 768
HEADS = 12
FF = 2048
BUCKETS = 32
MICRO = 2
INNER = 768


EPSILON = 1e-06
NEGATIVE = -1e30


def matmul(left_side, right_side):
    return jnp.dot(left_side, right_side, preferred_element_type=jnp.float32)


def matmul_tn(left_side, right_side):
    return lax.dot_general(
        left_side, right_side, (((0,), (0,)), ((), ())), preferred_element_type=jnp.float32
    )


def matmul_nt(left_side, right_side):
    return lax.dot_general(
        left_side, right_side, (((1,), (1,)), ((), ())), preferred_element_type=jnp.float32
    )


def split_heads(row_block):
    return row_block.reshape(row_block.shape[0], HEADS, row_block.shape[1] // HEADS)


def join_heads(head_block):
    return head_block.reshape(head_block.shape[0], head_block.shape[1] * head_block.shape[2])


def norm_forward(inputs, gain_row):
    factor = lax.rsqrt(jnp.mean(inputs * inputs, axis=-1, keepdims=True) + EPSILON)
    return (inputs * factor * gain_row, factor)


def norm_backward(inputs, factor, gain_row, upstream):
    scaled = gain_row * upstream
    inner_mean = jnp.mean(scaled * inputs, axis=-1, keepdims=True)
    input_grad = factor * (scaled - inputs * factor * factor * inner_mean)
    return (input_grad, jnp.sum(upstream * inputs * factor, axis=0))


def raw_scores(query_rows, key_rows, position_bias, causal):
    scores = (
        jnp.einsum(
            "qhd,khd->hqk",
            split_heads(query_rows),
            split_heads(key_rows),
            preferred_element_type=jnp.float32,
        )
        + position_bias
    )
    if causal:
        length = scores.shape[1]
        row_ids = lax.broadcasted_iota(jnp.int32, (length, length), 0)
        col_ids = lax.broadcasted_iota(jnp.int32, (length, length), 1)
        scores = jnp.where((col_ids <= row_ids)[None], scores, NEGATIVE)
    return scores


def attend_forward(query_rows, key_rows, value_rows, position_bias, causal):
    scores = raw_scores(query_rows, key_rows, position_bias, causal)
    row_max = jnp.max(scores, axis=-1, keepdims=True)
    powered = jnp.exp(scores - row_max)
    row_total = jnp.sum(powered, axis=-1, keepdims=True)
    prob_rows = (powered / row_total).astype(jnp.bfloat16)
    mixed_rows = jnp.einsum(
        "hqk,khd->qhd", prob_rows, split_heads(value_rows), preferred_element_type=jnp.float32
    )
    return (join_heads(mixed_rows).astype(jnp.bfloat16), row_max + jnp.log(row_total))


def attend_backward(query_rows, key_rows, value_rows, log_total, upstream, position_bias, causal):
    prob_rows = jnp.exp(raw_scores(query_rows, key_rows, position_bias, causal) - log_total)
    up_heads = split_heads(upstream)
    prob_grad = jnp.einsum(
        "qhd,khd->hqk", up_heads, split_heads(value_rows), preferred_element_type=jnp.float32
    )
    value_grad = jnp.einsum(
        "hqk,qhd->khd", prob_rows.astype(jnp.bfloat16), up_heads, preferred_element_type=jnp.float32
    )
    score_grad = (
        prob_rows * (prob_grad - jnp.sum(prob_rows * prob_grad, axis=-1, keepdims=True))
    ).astype(jnp.bfloat16)
    query_grad = jnp.einsum(
        "hqk,khd->qhd", score_grad, split_heads(key_rows), preferred_element_type=jnp.float32
    )
    key_grad = jnp.einsum(
        "hqk,qhd->khd", score_grad, split_heads(query_rows), preferred_element_type=jnp.float32
    )
    return (
        join_heads(query_grad).astype(jnp.bfloat16),
        join_heads(key_grad).astype(jnp.bfloat16),
        join_heads(value_grad).astype(jnp.bfloat16),
        score_grad,
    )


def bucket_onehot(bucket_block):
    return (bucket_block[:, :, None] == lax.broadcasted_iota(jnp.int32, (1, 1, BUCKETS), 2)).astype(
        jnp.bfloat16
    )


def expand_bias(bias_table, buckets):
    length = buckets.shape[0]
    block_rows = min(length, 128)
    blocks = buckets.reshape(length // block_rows, block_rows, length)

    def expand_block(bucket_block):
        return jnp.einsum(
            "ijb,bh->hij",
            bucket_onehot(bucket_block),
            bias_table,
            preferred_element_type=jnp.float32,
        )

    pieces = lax.map(expand_block, blocks)
    return jnp.transpose(pieces, (1, 0, 2, 3)).reshape(HEADS, length, length)


def shrink_bias(score_grad, buckets):
    length = buckets.shape[0]
    block_rows = min(length, 128)

    def shrink_block(block_index, running):
        start = block_index * block_rows
        bucket_block = lax.dynamic_slice_in_dim(buckets, start, block_rows, 0)
        grad_block = lax.dynamic_slice_in_dim(score_grad, start, block_rows, 2)
        return running + jnp.einsum(
            "shij,ijb->bh",
            grad_block,
            bucket_onehot(bucket_block),
            preferred_element_type=jnp.float32,
        )

    return lax.fori_loop(
        0, length // block_rows, shrink_block, jnp.zeros((BUCKETS, HEADS), jnp.float32)
    )


def shaped(flat_values):
    target_shapes = (
        (D, INNER),
        (D, INNER),
        (D, INNER),
        (INNER, D),
        (D, INNER),
        (D, INNER),
        (D, INNER),
        (INNER, D),
        (D, FF),
        (D, FF),
        (FF, D),
    )
    return tuple(
        (weight.reshape(target_shape) for weight, target_shape in zip(flat_values, target_shapes))
    )


def forward_weights(shards):
    (
        self_query,
        self_key,
        self_value,
        self_out,
        cross_query,
        cross_key,
        cross_value,
        cross_out,
        ff_gate,
        ff_up,
        ff_down,
    ) = shards
    return (
        lax.all_gather(self_query, "fsdp", axis=0, tiled=True),
        lax.all_gather(self_key, "fsdp", axis=0, tiled=True),
        lax.all_gather(self_value, "fsdp", axis=0, tiled=True),
        lax.all_gather(self_out, "fsdp", axis=0, tiled=True),
        lax.all_gather(cross_query, "fsdp", axis=0, tiled=True),
        lax.all_gather(cross_key, "fsdp", axis=0, tiled=True),
        lax.all_gather(cross_value, "fsdp", axis=0, tiled=True),
        lax.all_gather(cross_out, "fsdp", axis=0, tiled=True),
        lax.all_gather(ff_gate, "fsdp", axis=0, tiled=True),
        lax.all_gather(ff_up, "fsdp", axis=0, tiled=True),
        lax.all_gather(ff_down, "fsdp", axis=0, tiled=True),
    )


def backward_weights(shards):
    (
        self_query,
        self_key,
        self_value,
        self_out,
        cross_query,
        cross_key,
        cross_value,
        cross_out,
        ff_gate,
        ff_up,
        ff_down,
    ) = shards
    return (
        lax.all_gather(self_query, "fsdp", axis=0, tiled=True),
        lax.all_gather(self_key, "fsdp", axis=0, tiled=True),
        lax.all_gather(self_value, "fsdp", axis=0, tiled=True),
        lax.all_gather(self_out, "fsdp", axis=0, tiled=True),
        lax.all_gather(cross_query, "fsdp", axis=0, tiled=True),
        lax.all_gather(cross_key, "fsdp", axis=0, tiled=True),
        lax.all_gather(cross_value, "fsdp", axis=0, tiled=True),
        lax.all_gather(cross_out, "fsdp", axis=0, tiled=True),
        lax.all_gather(ff_gate, "fsdp", axis=0, tiled=True),
        lax.all_gather(ff_up, "fsdp", axis=0, tiled=True),
        lax.all_gather(ff_down, "fsdp", axis=0, tiled=True),
    )


def scatter_end(flat_grads):
    (
        self_query,
        self_key,
        self_value,
        self_out,
        cross_query,
        cross_key,
        cross_value,
        cross_out,
        ff_gate,
        ff_up,
        ff_down,
    ) = flat_grads
    return (
        lax.psum_scatter(self_query, "fsdp", scatter_dimension=0, tiled=True),
        lax.psum_scatter(self_key, "fsdp", scatter_dimension=0, tiled=True),
        lax.psum_scatter(self_value, "fsdp", scatter_dimension=0, tiled=True),
        lax.psum_scatter(self_out, "fsdp", scatter_dimension=0, tiled=True),
        lax.psum_scatter(cross_query, "fsdp", scatter_dimension=0, tiled=True),
        lax.psum_scatter(cross_key, "fsdp", scatter_dimension=0, tiled=True),
        lax.psum_scatter(cross_value, "fsdp", scatter_dimension=0, tiled=True),
        lax.psum_scatter(cross_out, "fsdp", scatter_dimension=0, tiled=True),
        lax.psum_scatter(ff_gate, "fsdp", scatter_dimension=0, tiled=True),
        lax.psum_scatter(ff_up, "fsdp", scatter_dimension=0, tiled=True),
        lax.psum_scatter(ff_down, "fsdp", scatter_dimension=0, tiled=True),
    )


def forward_pass(token_rows, encoder_rows, matrices, gain_values, position_bias, seq_count):
    (
        self_query,
        self_key,
        self_value,
        self_out,
        cross_query,
        cross_key,
        cross_value,
        cross_out,
        ff_gate,
        ff_up,
        ff_down,
    ) = matrices

    def by_sequence(row_block):
        return row_block.reshape(seq_count, row_block.shape[0] // seq_count, row_block.shape[1])

    inputs = token_rows.astype(jnp.float32)
    normed, factor_one = norm_forward(inputs, gain_values[0])
    normed_one = normed.astype(jnp.bfloat16)
    query_one = matmul(normed_one, self_query).astype(jnp.bfloat16)
    key_one = matmul(normed_one, self_key).astype(jnp.bfloat16)
    value_one = matmul(normed_one, self_value).astype(jnp.bfloat16)
    mixed_one, log_one = jax.vmap(partial(attend_forward, causal=True), in_axes=(0, 0, 0, None))(
        by_sequence(query_one), by_sequence(key_one), by_sequence(value_one), position_bias
    )
    mixed_one = mixed_one.reshape(inputs.shape[0], -1)
    middle = inputs + matmul(mixed_one, self_out)
    normed, factor_two = norm_forward(middle, gain_values[1])
    normed_two = normed.astype(jnp.bfloat16)
    query_two = matmul(normed_two, cross_query).astype(jnp.bfloat16)
    key_two = matmul(encoder_rows, cross_key).astype(jnp.bfloat16)
    value_two = matmul(encoder_rows, cross_value).astype(jnp.bfloat16)
    mixed_two, log_two = jax.vmap(partial(attend_forward, causal=False), in_axes=(0, 0, 0, None))(
        by_sequence(query_two), by_sequence(key_two), by_sequence(value_two), jnp.float32(0.0)
    )
    mixed_two = mixed_two.reshape(inputs.shape[0], -1)
    late = middle + matmul(mixed_two, cross_out)
    normed, factor_three = norm_forward(late, gain_values[2])
    normed_three = normed.astype(jnp.bfloat16)
    gate_rows = matmul(normed_three, ff_gate)
    up_rows = matmul(normed_three, ff_up)
    hidden = (jax.nn.gelu(gate_rows, approximate=True) * up_rows).astype(jnp.bfloat16)
    result_rows = (late + matmul(hidden, ff_down)).astype(jnp.bfloat16)
    saved = (
        inputs,
        factor_one,
        normed_one,
        query_one,
        key_one,
        value_one,
        mixed_one,
        log_one,
        middle,
        factor_two,
        normed_two,
        query_two,
        key_two,
        value_two,
        mixed_two,
        log_two,
        late,
        factor_three,
        normed_three,
        gate_rows,
        up_rows,
        hidden,
    )
    return (result_rows, saved)


def backward_pass(
    encoder_rows, cotangent, matrices, gain_values, position_bias, buckets, saved, seq_count
):
    (
        self_query,
        self_key,
        self_value,
        self_out,
        cross_query,
        cross_key,
        cross_value,
        cross_out,
        ff_gate,
        ff_up,
        ff_down,
    ) = matrices
    (
        inputs,
        factor_one,
        normed_one,
        query_one,
        key_one,
        value_one,
        mixed_one,
        log_one,
        middle,
        factor_two,
        normed_two,
        query_two,
        key_two,
        value_two,
        mixed_two,
        log_two,
        late,
        factor_three,
        normed_three,
        gate_rows,
        up_rows,
        hidden,
    ) = saved

    def by_sequence(row_block):
        return row_block.reshape(seq_count, row_block.shape[0] // seq_count, row_block.shape[1])

    def flat_rows(seq_block):
        return seq_block.reshape(seq_block.shape[0] * seq_block.shape[1], seq_block.shape[2])

    grad_ff_down = matmul_tn(hidden, cotangent)
    hidden_grad = matmul_nt(cotangent, ff_down)
    activated, gelu_pull = jax.vjp(
        lambda gate_values: jax.nn.gelu(gate_values, approximate=True), gate_rows
    )
    gate_grad = gelu_pull(hidden_grad * up_rows)[0].astype(jnp.bfloat16)
    up_grad = (hidden_grad * activated).astype(jnp.bfloat16)
    grad_ff_gate = matmul_tn(normed_three, gate_grad)
    grad_ff_up = matmul_tn(normed_three, up_grad)
    normed_grad = matmul_nt(gate_grad, ff_gate) + matmul_nt(up_grad, ff_up)
    norm_grad, gain_three = norm_backward(late, factor_three, gain_values[2], normed_grad)
    late_grad = cotangent.astype(jnp.float32) + norm_grad
    branch_grad = late_grad.astype(jnp.bfloat16)
    grad_cross_out = matmul_tn(mixed_two, branch_grad)
    mixed_grad = matmul_nt(branch_grad, cross_out).astype(jnp.bfloat16)
    query_grad, key_grad, value_grad, _ = jax.vmap(
        partial(attend_backward, causal=False), in_axes=(0, 0, 0, 0, 0, None)
    )(
        by_sequence(query_two),
        by_sequence(key_two),
        by_sequence(value_two),
        log_two,
        by_sequence(mixed_grad),
        jnp.float32(0.0),
    )
    query_grad = flat_rows(query_grad)
    key_grad = flat_rows(key_grad)
    value_grad = flat_rows(value_grad)
    grad_cross_query = matmul_tn(normed_two, query_grad)
    grad_cross_key = matmul_tn(encoder_rows, key_grad)
    grad_cross_value = matmul_tn(encoder_rows, value_grad)
    encoder_grad = (matmul_nt(key_grad, cross_key) + matmul_nt(value_grad, cross_value)).astype(
        jnp.bfloat16
    )
    norm_grad, gain_two = norm_backward(
        middle, factor_two, gain_values[1], matmul_nt(query_grad, cross_query)
    )
    middle_grad = late_grad + norm_grad
    branch_grad = middle_grad.astype(jnp.bfloat16)
    grad_self_out = matmul_tn(mixed_one, branch_grad)
    mixed_grad = matmul_nt(branch_grad, self_out).astype(jnp.bfloat16)
    query_grad, key_grad, value_grad, score_grad = jax.vmap(
        partial(attend_backward, causal=True), in_axes=(0, 0, 0, 0, 0, None)
    )(
        by_sequence(query_one),
        by_sequence(key_one),
        by_sequence(value_one),
        log_one,
        by_sequence(mixed_grad),
        position_bias,
    )
    table_part = shrink_bias(score_grad, buckets)
    query_grad = flat_rows(query_grad)
    key_grad = flat_rows(key_grad)
    value_grad = flat_rows(value_grad)
    grad_self_query = matmul_tn(normed_one, query_grad)
    grad_self_key = matmul_tn(normed_one, key_grad)
    grad_self_value = matmul_tn(normed_one, value_grad)
    normed_grad = (
        matmul_nt(query_grad, self_query)
        + matmul_nt(key_grad, self_key)
        + matmul_nt(value_grad, self_value)
    )
    norm_grad, gain_one = norm_backward(inputs, factor_one, gain_values[0], normed_grad)
    input_grad = (middle_grad + norm_grad).astype(jnp.bfloat16)
    weight_grads = (
        grad_self_query,
        grad_self_key,
        grad_self_value,
        grad_self_out,
        grad_cross_query,
        grad_cross_key,
        grad_cross_value,
        grad_cross_out,
        grad_ff_gate,
        grad_ff_up,
        grad_ff_down,
    )
    return (
        input_grad,
        encoder_grad,
        weight_grads,
        jnp.stack([gain_one, gain_two, gain_three]),
        table_part,
    )


def per_device(
    tokens,
    encoder_states,
    self_query,
    self_key,
    self_value,
    self_out,
    cross_query,
    cross_key,
    cross_value,
    cross_out,
    ff_gate,
    ff_up,
    ff_down,
    norm_gains,
    bias_table,
    buckets,
    cotangent,
):
    shards = (
        self_query,
        self_key,
        self_value,
        self_out,
        cross_query,
        cross_key,
        cross_value,
        cross_out,
        ff_gate,
        ff_up,
        ff_down,
    )
    gain_values = norm_gains.astype(jnp.float32)
    position_bias = expand_bias(bias_table, buckets)
    length = buckets.shape[0]
    token_count = tokens.shape[0] // MICRO
    encoder_count = encoder_states.shape[0] // MICRO
    seq_count = token_count // length
    outputs = []
    token_grads = []
    encoder_grads = []
    summed = None
    gains_sum = jnp.zeros_like(gain_values)
    table_sum = jnp.zeros((BUCKETS, HEADS), jnp.float32)
    for micro_index in range(MICRO):
        token_rows = tokens[micro_index * token_count : (micro_index + 1) * token_count]
        encoder_rows = encoder_states[
            micro_index * encoder_count : (micro_index + 1) * encoder_count
        ]
        cotangent_rows = cotangent[micro_index * token_count : (micro_index + 1) * token_count]
        forward_matrices = shaped(forward_weights(shards))
        result_rows, saved = forward_pass(
            token_rows, encoder_rows, forward_matrices, gain_values, position_bias, seq_count
        )
        backward_matrices = shaped(backward_weights(shards))
        input_grad, encoder_grad, weight_grads, gain_grad, table_part = backward_pass(
            encoder_rows,
            cotangent_rows,
            backward_matrices,
            gain_values,
            position_bias,
            buckets,
            saved,
            seq_count,
        )
        outputs.append(result_rows)
        token_grads.append(input_grad)
        encoder_grads.append(encoder_grad)
        gains_sum = gains_sum + gain_grad
        table_sum = table_sum + table_part
        flat_grads = tuple((one_grad.reshape(-1) for one_grad in weight_grads))
        summed = (
            flat_grads
            if summed is None
            else tuple((first + second for first, second in zip(summed, flat_grads)))
        )
    rounded = tuple((one_grad.astype(jnp.bfloat16).astype(jnp.float32) for one_grad in summed))
    owned_sums = scatter_end(rounded)
    gains_grad, table_grad = lax.psum((gains_sum, table_sum), "fsdp")
    return (
        jnp.concatenate(outputs, axis=0),
        jnp.concatenate(token_grads, axis=0),
        jnp.concatenate(encoder_grads, axis=0),
        owned_sums[0],
        owned_sums[1],
        owned_sums[2],
        owned_sums[3],
        owned_sums[4],
        owned_sums[5],
        owned_sums[6],
        owned_sums[7],
        owned_sums[8],
        owned_sums[9],
        owned_sums[10],
        gains_grad,
        table_grad,
    )


def solution(mesh):
    return jax.shard_map(
        per_device,
        mesh=mesh,
        in_specs=(
            P("fsdp", None),
            P("fsdp", None),
            P("fsdp"),
            P("fsdp"),
            P("fsdp"),
            P("fsdp"),
            P("fsdp"),
            P("fsdp"),
            P("fsdp"),
            P("fsdp"),
            P("fsdp"),
            P("fsdp"),
            P("fsdp"),
            P(),
            P(),
            P(),
            P("fsdp", None),
        ),
        out_specs=(
            P("fsdp", None),
            P("fsdp", None),
            P("fsdp", None),
            P("fsdp"),
            P("fsdp"),
            P("fsdp"),
            P("fsdp"),
            P("fsdp"),
            P("fsdp"),
            P("fsdp"),
            P("fsdp"),
            P("fsdp"),
            P("fsdp"),
            P("fsdp"),
            P(),
            P(),
        ),
        check_vma=False,
    )
```

profile of v0, /device:TPU:0, one launch (start us, length us, event | category | flops | bytes accessed | tf_op | source)
XLA Modules:
  0.0 1523.2 jit_solution(11859664838659002291)
XLA Ops:
  16.7 17.4 %while.38 = (s32[]{:T(128)}, f32[4,12,128,512]{3,1,2,0:T(8,128)}, s32[4,128,512]{2,1,0:T(8,128)}, bf16[32,12]{0,1:T(8,128)(2,1)S(1)}, s32[]{:T(128)}) while((s32[]{:T(128)}, f32[4,12,128,512]{3,1,2,0:T(8,128)}, s32[4,128,512]{2,1,0:T(8,128)}, bf16[32,12]{0,1:T(8,128)(2,1)S(1)}, s32[]{:T(128)}) %tuple.158), condition=%wide.region_2.3_spmd, body=%wide.region_1.2_spmd.sunk | while | flops 52428800 | bytes 4981581 | solution.py:131
  34.1 17.7 %copy.174 = f32[12,512,512]{1,2,0:T(8,128)} copy(f32[12,512,512]{2,0,1:T(8,128)} %bitcast.309) | data formatting | bytes 25165824 | tf_op jit(solution)/shard_map/vmap()/broadcast_in_dim;reshape | solution.py:58
  51.8 15.9 %all-gather.14.cloned.1.call-done = bf16[589824]{0:T(1024)(128)(2,1)} async-done(((bf16[18432]{0:T(1024)(128)(2,1)}), bf16[589824]{0:T(1024)(128)(2,1)}) %all-gather.14.cloned.1.call-update) | async-done | bytes 1179664 | tf_op jit(solution)/shard_map/all_gather | solution.py:189
  72.1 51.5 %all-gather.16.cloned.1.call-done = bf16[589824]{0:T(1024)(128)(2,1)} async-done(((bf16[18432]{0:T(1024)(128)(2,1)}), bf16[589824]{0:T(1024)(128)(2,1)}) %all-gather.16.cloned.1.call-update) | async-done | bytes 1179664 | tf_op jit(solution)/shard_map/all_gather | solution.py:190
  133.3 46.2 %all-gather.12.cloned.1.call-done = bf16[589824]{0:T(1024)(128)(2,1)} async-done(((bf16[18432]{0:T(1024)(128)(2,1)}), bf16[589824]{0:T(1024)(128)(2,1)}) %all-gather.12.cloned.1.call-update) | async-done | bytes 1179664 | tf_op jit(solution)/shard_map/all_gather | solution.py:191
  185.5 49.7 %all-gather.20.cloned.1.call-done = bf16[589824]{0:T(1024)(128)(2,1)} async-done(((bf16[18432]{0:T(1024)(128)(2,1)}), bf16[589824]{0:T(1024)(128)(2,1)}) %all-gather.20.cloned.1.call-update) | async-done | bytes 1179664 | tf_op jit(solution)/shard_map/all_gather | solution.py:195
  243.3 47.7 %all-gather.24.cloned.1.call-done = bf16[589824]{0:T(1024)(128)(2,1)} async-done(((bf16[18432]{0:T(1024)(128)(2,1)}), bf16[589824]{0:T(1024)(128)(2,1)}) %all-gather.24.cloned.1.call-update) | async-done | bytes 1179664 | tf_op jit(solution)/shard_map/all_gather | solution.py:194
  319.0 6.1 fusion.149
  332.9 13.9 all-gather.18.cloned.1.call-done
  352.6 50.1 %all-gather.22.cloned.1.call-done = bf16[589824]{0:T(1024)(128)(2,1)} async-done(((bf16[18432]{0:T(1024)(128)(2,1)}), bf16[589824]{0:T(1024)(128)(2,1)}) %all-gather.22.cloned.1.call-update) | async-done | bytes 1179664 | tf_op jit(solution)/shard_map/all_gather | solution.py:193
  411.7 7.3 fusion.151
  441.2 17.4 %all-gather.26.cloned.1.call-done = bf16[589824]{0:T(1024)(128)(2,1)} async-done(((bf16[18432]{0:T(1024)(128)(2,1)}), bf16[589824]{0:T(1024)(128)(2,1)}) %all-gather.26.cloned.1.call-update) | async-done | bytes 1179664 | tf_op jit(solution)/shard_map/all_gather | solution.py:196
  478.4 41.0 %all-gather.28.cloned.1.call-done = bf16[1572864]{0:T(1024)(128)(2,1)} async-done(((bf16[49152]{0:T(1024)(128)(2,1)}), bf16[1572864]{0:T(1024)(128)(2,1)}) %all-gather.28.cloned.1.call-update) | async-done | bytes 3145744 | tf_op jit(solution)/shard_map/all_gather | solution.py:197
  519.3 5.8 reshape.742
  525.2 54.7 %all-gather.30.cloned.1.call-done = bf16[1572864]{0:T(1024)(128)(2,1)} async-done(((bf16[49152]{0:T(1024)(128)(2,1)}), bf16[1572864]{0:T(1024)(128)(2,1)}) %all-gather.30.cloned.1.call-update) | async-done | bytes 3145744 | tf_op jit(solution)/shard_map/all_gather | solution.py:198
  579.8 5.8 reshape.743
  585.6 6.0 fusion.154
  595.4 45.1 %all-gather.32.cloned.1.call-done = bf16[1572864]{0:T(1024)(128)(2,1)} async-done(((bf16[49152]{0:T(1024)(128)(2,1)}), bf16[1572864]{0:T(1024)(128)(2,1)}) %all-gather.32.cloned.1.call-update) | async-done | bytes 3145744 | tf_op jit(solution)/shard_map/all_gather | solution.py:199
  640.5 6.8 reshape.744
  647.3 9.4 multiply_convert_fusion.5
  658.6 4.4 fusion.165
  663.0 4.5 fusion.166
  675.8 7.3 multiply_convert_fusion.4
  697.0 7.9 fusion.96
  704.9 9.0 multiply_reduce_fusion.1
  713.9 6.9 multiply_convert_fusion.1
  728.0 7.9 fusion.90
  736.0 9.0 multiply_reduce_fusion.3
  744.9 7.1 multiply_convert_fusion.3
  766.6 7.7 fusion.93
  774.2 9.0 multiply_reduce_fusion.2
  783.2 7.3 multiply_convert_fusion.2
  800.8 7.9 fusion.99
  808.7 9.0 multiply_reduce_fusion
  817.7 7.1 multiply_convert_fusion
  837.7 4.0 copy.177
  841.7 4.1 copy.178
  845.9 4.6 fusion.59
  850.5 7.0 reshape.765
  857.6 4.6 fusion.89
  887.1 4.3 fusion.88
  894.7 3.8 fusion.87
  918.1 4.1 fusion.84
  936.7 34.4 %while.39 = (s32[]{:T(128)}, f32[32,12]{0,1:T(8,128)S(1)}, s32[512,512]{1,0:T(8,128)}, bf16[1,12,512,512]{2,3,1,0:T(8,128)(2,1)}, s32[]{:T(128)}, /*index=5*/s32[]{:T(128)}, s32[]{:T(128)}, s32[]{:T(128)}) while((s32[]{:T(128)}, f32[32,12]{0,1:T(8,128)S(1)}, s32[512,512]{1,0:T(8,128)}, bf16[1,12,512,512]{2,3,1,0:T(8,128)(2,1)}, ...), condition=%wide.region_45.46_spmd.clone, body=%wide.region_44.45_spmd.clone.sunk | while | flops 52429576 | bytes 8653981 | solution.py:150
  971.2 34.5 %while.40 = (s32[]{:T(128)}, f32[32,12]{0,1:T(8,128)S(1)}, s32[512,512]{1,0:T(8,128)}, bf16[1,12,512,512]{2,3,1,0:T(8,128)(2,1)}, s32[]{:T(128)}, /*index=5*/s32[]{:T(128)}, s32[]{:T(128)}, s32[]{:T(128)}) while((s32[]{:T(128)}, f32[32,12]{0,1:T(8,128)S(1)}, s32[512,512]{1,0:T(8,128)}, bf16[1,12,512,512]{2,3,1,0:T(8,128)(2,1)}, ...), condition=%wide.region_47.48_spmd.clone, body=%wide.region_46.47_spmd.clone.sunk | while | flops 52429576 | bytes 8653981 | solution.py:150
  1005.7 40.4 %all-reduce.11 = (f32[3,768]{1,0:T(4,128)}, f32[32,12]{0,1:T(8,128)}) all-reduce(f32[3,768]{1,0:T(4,128)S(1)} %maximum_add_fusion, f32[32,12]{0,1:T(8,128)S(1)} %add.359), channel_id=1, replica_groups=mesh['fsdp'=32] {'fsdp'}, use_global_device_ids=true, to_apply=%region_43.44 | all-reduce | flops 2688 | bytes 21504 | tf_op jit(solution)/shard_map/psum | solution.py:545
  1046.1 5.0 add_convert_fusion.14
  1065.2 434.0 %all-reduce.15.cloned.1.call-done = (f32[589824]{0:T(1024)}, f32[589824]{0:T(1024)}, f32[589824]{0:T(1024)}, f32[589824]{0:T(1024)}, f32[589824]{0:T(1024)}, /*i...) async-done(((f32[589824]{0:T(1024)}, f32[589824]{0:T(1024)}, f32[589824]{0:T(1024)}, ...) | async-done | bytes 37748752
  (513 shorter events, 381.3 us)
Async XLA Ops:
  7.2 9.4 copy-start.125
  7.2 9.5 copy-start.116
  7.2 60.5 %all-gather.14.cloned.1.call-start = ((), (), s32[]{:S(2)}) async-start(), calls=%async_computation.1 | async-start | bytes 1216512 | tf_op jit(solution)/shard_map/all_gather | solution.py:189
  7.9 115.7 %all-gather.16.cloned.1.call-start = ((), (), s32[]{:S(2)}) async-start(), calls=%async_computation.2 | async-start | bytes 1216512 | tf_op jit(solution)/shard_map/all_gather | solution.py:190
  8.7 170.8 %all-gather.12.cloned.1.call-start = ((), (), s32[]{:S(2)}) async-start(), calls=%async_computation | async-start | bytes 1216512 | tf_op jit(solution)/shard_map/all_gather | solution.py:191
  9.4 225.8 %all-gather.20.cloned.1.call-start = ((), (), s32[]{:S(2)}) async-start(), calls=%async_computation.4 | async-start | bytes 1216512 | tf_op jit(solution)/shard_map/all_gather | solution.py:195
  10.0 281.0 %all-gather.24.cloned.1.call-start = ((), (), s32[]{:S(2)}) async-start(), calls=%async_computation.6 | async-start | bytes 1216512 | tf_op jit(solution)/shard_map/all_gather | solution.py:194
  10.6 336.2 %all-gather.18.cloned.1.call-start = ((), (), s32[]{:S(2)}) async-start(), calls=%async_computation.3 | async-start | bytes 1216512 | tf_op jit(solution)/shard_map/all_gather | solution.py:192
  11.2 391.5 %all-gather.22.cloned.1.call-start = ((), (), s32[]{:S(2)}) async-start(), calls=%async_computation.5 | async-start | bytes 1216512 | tf_op jit(solution)/shard_map/all_gather | solution.py:193
  11.9 446.6 %all-gather.26.cloned.1.call-start = ((), (), s32[]{:S(2)}) async-start(), calls=%async_computation.7 | async-start | bytes 1216512 | tf_op jit(solution)/shard_map/all_gather | solution.py:196
  12.7 506.7 %all-gather.28.cloned.1.call-start = ((), (), s32[]{:S(2)}) async-start(), calls=%async_computation.8 | async-start | bytes 3244032 | tf_op jit(solution)/shard_map/all_gather | solution.py:197
  13.4 566.4 %all-gather.30.cloned.1.call-start = ((), (), s32[]{:S(2)}) async-start(), calls=%async_computation.9 | async-start | bytes 3244032 | tf_op jit(solution)/shard_map/all_gather | solution.py:198
  14.0 626.5 %all-gather.32.cloned.1.call-start = ((), (), s32[]{:S(2)}) async-start(), calls=%async_computation.10 | async-start | bytes 3244032 | tf_op jit(solution)/shard_map/all_gather | solution.py:199
  14.7 1484.4 %all-reduce.15.cloned.1.call-start = ((), (), s32[]{:S(2)}) async-start(), calls=%async_computation.11 | async-start | bytes 75497472
  16.7 167.1 %copy-start.112 = (f32[768]{0:T(1024)}, f32[768]{0:T(1024)S(1)}, u32[]{:S(2)}) copy-start(f32[768]{0:T(1024)S(1)} %get-tuple-element.271) | copy-start | bytes 9220
  16.7 410.3 %copy-start.114 = (f32[768]{0:T(1024)}, f32[768]{0:T(1024)S(1)}, u32[]{:S(2)}) copy-start(f32[768]{0:T(1024)S(1)} %get-tuple-element.270) | copy-start | bytes 9220
  51.8 18.5 %copy-start.6 = (bf16[1024,768]{1,0:T(8,128)(2,1)S(1)}, bf16[1024,768]{1,0:T(8,128)(2,1)}, u32[]{:S(2)}) copy-start(bf16[1024,768]{1,0:T(8,128)(2,1)} %param.23) | copy-start | bytes 4718596
  51.8 130.3 %copy-start.117 = (f32[512]{0:T(512)}, f32[512]{0:T(512)S(1)}, u32[]{:S(2)}) copy-start(f32[512]{0:T(512)S(1)} %get-tuple-element.350) | copy-start | bytes 6148
  51.8 132.0 %copy-start.119 = (f32[512]{0:T(512)}, f32[512]{0:T(512)S(1)}, u32[]{:S(2)}) copy-start(f32[512]{0:T(512)S(1)} %get-tuple-element.351) | copy-start | bytes 6148
  70.3 59.6 %copy-start.99 = (bf16[768,768]{1,0:T(8,128)(2,1)}, bf16[768,768]{1,0:T(8,128)(2,1)S(1)}, u32[]{:S(2)}) copy-start(bf16[768,768]{1,0:T(8,128)(2,1)S(1)} %reshape.729) | copy-start | bytes 3538948
  185.5 53.1 %copy-start.49 = (bf16[1024,768]{1,0:T(8,128)(2,1)S(1)}, bf16[1024,768]{1,0:T(8,128)(2,1)}, u32[]{:S(2)}) copy-start(bf16[1024,768]{1,0:T(8,128)(2,1)} %param.24) | copy-start | bytes 4718596
  305.5 13.5 copy-start.33
  307.2 11.8 copy-start.20
  352.6 56.8 %copy-start.121 = (f32[512]{0:T(512)}, f32[512]{0:T(512)S(1)}, u32[]{:S(2)}) copy-start(f32[512]{0:T(512)S(1)} %add_rsqrt_fusion.1) | copy-start | bytes 6148
  441.2 20.7 %copy-start.13 = (f32[512,768]{1,0:T(8,128)S(1)}, f32[512,768]{1,0:T(8,128)}, u32[]{:S(2)}) copy-start(f32[512,768]{1,0:T(8,128)} %copy-done.12) | copy-start | bytes 4718596
  464.4 12.8 copy-start.16
  647.3 9.4 copy-start.77
  696.9 7.9 copy-start.30
  696.9 7.9 copy-start.69
  697.0 16.9 %slice-start.9 = ((s8[12582912]{0:T(1024)(128)(4,1)}), s8[4194304]{0:T(1024)(128)(4,1)S(1)}, s32[]{:S(2)}) async-start(s8[12582912]{0:T(1024)(128)(4,1)} %bitcast.299), calls=%async_computation.21 | async-start | bytes 8388608
  697.0 16.9 %slice-start.10 = ((s8[12582912]{0:T(1024)(128)(4,1)}), s8[4194304]{0:T(1024)(128)(4,1)S(1)}, s32[]{:S(2)}) async-start(s8[12582912]{0:T(1024)(128)(4,1)} %bitcast.299), calls=%async_computation.22 | async-start | bytes 8388608
  704.9 9.0 slice-start.11
  728.0 7.9 copy-start.31
  728.0 7.9 copy-start.68
  728.0 16.9 %slice-start.6 = ((s8[12582912]{0:T(1024)(128)(4,1)}), s8[4194304]{0:T(1024)(128)(4,1)S(1)}, s32[]{:S(2)}) async-start(s8[12582912]{0:T(1024)(128)(4,1)} %bitcast.297), calls=%async_computation.18 | async-start | bytes 8388608
  728.0 16.9 %slice-start.7 = ((s8[12582912]{0:T(1024)(128)(4,1)}), s8[4194304]{0:T(1024)(128)(4,1)S(1)}, s32[]{:S(2)}) async-start(s8[12582912]{0:T(1024)(128)(4,1)} %bitcast.297), calls=%async_computation.19 | async-start | bytes 8388608
  736.0 9.0 slice-start.8
  766.5 7.7 copy-start.66
  766.6 16.7 %slice-start.3 = ((s8[12582912]{0:T(1024)(128)(4,1)}), s8[4194304]{0:T(1024)(128)(4,1)S(1)}, s32[]{:S(2)}) async-start(s8[12582912]{0:T(1024)(128)(4,1)} %bitcast.295), calls=%async_computation.15 | async-start | bytes 8388608
  766.6 16.7 %slice-start.4 = ((s8[12582912]{0:T(1024)(128)(4,1)}), s8[4194304]{0:T(1024)(128)(4,1)S(1)}, s32[]{:S(2)}) async-start(s8[12582912]{0:T(1024)(128)(4,1)} %bitcast.295), calls=%async_computation.16 | async-start | bytes 8388608
  774.2 9.0 slice-start.5
  796.8 97.9 %copy-start.8 = (f32[512,768]{1,0:T(8,128)}, f32[512,768]{1,0:T(8,128)S(1)}, u32[]{:S(2)}) copy-start(f32[512,768]{1,0:T(8,128)S(1)} %multiply_add_fusion) | copy-start | bytes 4718596
  800.8 7.9 copy-start.32
  800.8 7.9 copy-start.64
  800.8 16.9 %slice-start = ((s8[12582912]{0:T(1024)(128)(4,1)}), s8[4194304]{0:T(1024)(128)(4,1)S(1)}, s32[]{:S(2)}) async-start(s8[12582912]{0:T(1024)(128)(4,1)} %bitcast.293), calls=%async_computation.12 | async-start | bytes 8388608
  800.8 16.9 %slice-start.1 = ((s8[12582912]{0:T(1024)(128)(4,1)}), s8[4194304]{0:T(1024)(128)(4,1)S(1)}, s32[]{:S(2)}) async-start(s8[12582912]{0:T(1024)(128)(4,1)} %bitcast.293), calls=%async_computation.13 | async-start | bytes 8388608
  808.7 9.0 slice-start.2
  824.8 8.3 slice-start.14
  (108 other events, 304.3 us)
Sparse Core Ops, SparseCore 0:
  10.9 56.7 all-gather.13
  70.6 52.9 all-gather.15
  126.5 52.9 all-gather.11
  182.3 52.9 all-gather.19
  238.0 52.9 all-gather.23
  293.8 52.9 all-gather.17
  349.7 52.9 all-gather.21
  405.6 52.9 all-gather.25
  461.4 57.8 all-gather.27
  522.0 57.7 all-gather.29
  582.7 57.7 all-gather.31
  925.9 573.2 all-reduce.14
where the time goes:
time: 1540 us; the launch traced here: 1520 us
  waiting for transfers between devices  874 us (57%)
  matrix products  318 us (21%)
  local copies, waits for them, and re-layouts  229 us (15%)
  other arithmetic  45.6 us (3%)
  blocking collectives  40.4 us (3%)
  between operations  15.9 us (1%)
    unnamed x13, waiting for transfers between devices  441 us
    dot_general x22, matrix products, matmul_tn(): lax.dot_general(left_side, right_side, (((0,), (0,)), ((), ())), preferre...  61 us
    dot_general x22, matrix products, matmul(): return jnp.dot(left_side, right_side, preferred_element_type=jnp.float32)  55.8 us
    all_gather x1, waiting for transfers between devices, forward_weights(): lax.all_gather(ff_up, 'fsdp', axis=0, tiled=True)  54.7 us
    all_gather x1, waiting for transfers between devices, forward_weights(): lax.all_gather(self_key, 'fsdp', axis=0, tiled=True)  51.5 us
    all_gather x1, waiting for transfers between devices, forward_weights(): lax.all_gather(cross_query, 'fsdp', axis=0, tiled=True)  50.1 us
    all_gather x1, waiting for transfers between devices, forward_weights(): lax.all_gather(cross_value, 'fsdp', axis=0, tiled=True)  49.7 us
    unnamed x301, local copies, waits for them, and re-layouts  48.7 us
  transfers between devices with their start and end apart: 12, of which 12 were waited for; matrix products, arithmetic and copies ran while one was open for 18% of the time, Pallas kernels for 0%

commit v1 on v0

v1 whole, which is shorter than its diff:
```python
from functools import partial

import jax
import jax.numpy as jnp
from jax import lax
from jax.experimental import pallas as pl
from jax.experimental.pallas import tpu as pltpu
from jax.sharding import PartitionSpec as P

D = 768
HEADS = 12
HD = 64
FF = 2048
BUCKETS = 32
INNER = 768
PAIRS = HEADS // 2
WIDE = 2 * HD

EPSILON = 1e-06
NEGATIVE = -1e30
VMEM_LIMIT = 48 * 1024 * 1024
F32 = jnp.float32
BF16 = jnp.bfloat16


def params():
    return pltpu.CompilerParams(vmem_limit_bytes=VMEM_LIMIT)


def matmul(left_side, right_side):
    return jnp.dot(left_side, right_side, preferred_element_type=F32)


def matmul_tn(left_side, right_side):
    return lax.dot_general(
        left_side, right_side, (((0,), (0,)), ((), ())), preferred_element_type=F32
    )


def matmul_nt(left_side, right_side):
    return lax.dot_general(
        left_side, right_side, (((1,), (1,)), ((), ())), preferred_element_type=F32
    )


def norm_factor(inputs):
    return lax.rsqrt(jnp.mean(inputs * inputs, axis=-1, keepdims=True) + EPSILON)


def norm_backward(inputs, factor, gain_row, upstream):
    scaled = gain_row * upstream
    inner_mean = jnp.mean(scaled * inputs, axis=-1, keepdims=True)
    input_grad = factor * (scaled - inputs * factor * factor * inner_mean)
    return (input_grad, jnp.sum(upstream * inputs * factor, axis=0))


BAND = 16


def bias_kernel(band_ref, out_ref):
    length = out_ref.shape[1]
    band = band_ref[0]
    for group in range(length // BAND):
        rolled = pltpu.roll(band, length + BAND * group, 1)
        out_ref[0, group * BAND : (group + 1) * BAND, :] = rolled[:, :length].astype(BF16)


def expand_bias(distance_bias, length):
    extended = jnp.concatenate(
        [jnp.full((HEADS, length), NEGATIVE, F32), distance_bias.astype(F32)], axis=1
    )
    rows = [
        jnp.pad(extended[:, : 2 * length - row], ((0, 0), (row, 0)), constant_values=NEGATIVE)
        for row in range(BAND)
    ]
    bands = jnp.stack(rows, axis=1)
    return pl.pallas_call(
        bias_kernel,
        grid=(HEADS,),
        in_specs=[pl.BlockSpec((1, BAND, 2 * length), lambda h: (h, 0, 0))],
        out_specs=pl.BlockSpec((1, length, length), lambda h: (h, 0, 0)),
        out_shape=jax.ShapeDtypeStruct((HEADS, length, length), BF16),
        compiler_params=params(),
        name="bias",
    )(bands)


def head_masks():
    lanes = lax.broadcasted_iota(jnp.int32, (1, WIDE), 1)
    low = (lanes < HD).astype(F32).astype(BF16)
    high = (lanes >= HD).astype(F32).astype(BF16)
    return (low, high)


def attend_core(queries, keys, values, bias_ref, out_ref, log_ref):
    length = queries.shape[0]
    causal = bias_ref is not None
    masks = head_masks()
    step = length // 2
    for part in range(2):
        begin, end = part * step, (part + 1) * step
        reach = end if causal else keys.shape[0]
        mixed = None
        for head in range(2):
            scores = matmul_nt(keys[:reach] * masks[head], queries[begin:end])
            if causal:
                scores = scores + bias_ref[head, :reach, begin:end].astype(F32)
            top = jnp.max(scores, axis=0, keepdims=True)
            powered = jnp.exp(scores - top)
            total = jnp.sum(powered, axis=0, keepdims=True)
            probs = (powered * (1.0 / total)).astype(BF16)
            term = matmul_tn(values[:reach] * masks[head], probs)
            mixed = term if mixed is None else mixed + term
            log_ref[0, 0, head : head + 1, begin:end] = top + jnp.log(total)
        out_ref[begin:end, :] = jnp.transpose(mixed).astype(BF16)


def self_forward_kernel(qkv_ref, bias_ref, out_ref, log_ref):
    attend_core(
        qkv_ref[:, :WIDE],
        qkv_ref[:, WIDE : 2 * WIDE],
        qkv_ref[:, 2 * WIDE :],
        bias_ref,
        out_ref,
        log_ref,
    )


def cross_forward_kernel(q_ref, kv_ref, out_ref, log_ref):
    attend_core(q_ref[...], kv_ref[:, :WIDE], kv_ref[:, WIDE:], None, out_ref, log_ref)


def self_forward(qkv, bias, length):
    seqs = qkv.shape[0] // length
    return pl.pallas_call(
        self_forward_kernel,
        grid=(PAIRS, seqs),
        in_specs=[
            pl.BlockSpec((length, 3 * WIDE), lambda p, s: (s, p)),
            pl.BlockSpec((2, length, length), lambda p, s: (p, 0, 0)),
        ],
        out_specs=[
            pl.BlockSpec((length, WIDE), lambda p, s: (s, p)),
            pl.BlockSpec((1, 1, 2, length), lambda p, s: (s, p, 0, 0)),
        ],
        out_shape=[
            jax.ShapeDtypeStruct((qkv.shape[0], INNER), BF16),
            jax.ShapeDtypeStruct((seqs, PAIRS, 2, length), F32),
        ],
        compiler_params=params(),
        cost_estimate=pl.CostEstimate(
            flops=40_000_000_000, bytes_accessed=16_000_000, transcendentals=6_000_000
        ),
        name="self_forward",
    )(qkv, bias)


def cross_forward(queries, kv, length):
    seqs = queries.shape[0] // length
    extent = kv.shape[0] // seqs
    return pl.pallas_call(
        cross_forward_kernel,
        grid=(PAIRS, seqs),
        in_specs=[
            pl.BlockSpec((length, WIDE), lambda p, s: (s, p)),
            pl.BlockSpec((extent, 2 * WIDE), lambda p, s: (s, p)),
        ],
        out_specs=[
            pl.BlockSpec((length, WIDE), lambda p, s: (s, p)),
            pl.BlockSpec((1, 1, 2, length), lambda p, s: (s, p, 0, 0)),
        ],
        out_shape=[
            jax.ShapeDtypeStruct((queries.shape[0], INNER), BF16),
            jax.ShapeDtypeStruct((seqs, PAIRS, 2, length), F32),
        ],
        compiler_params=params(),
        cost_estimate=pl.CostEstimate(
            flops=40_000_000_000, bytes_accessed=16_000_000, transcendentals=6_000_000
        ),
        name="cross_forward",
    )(queries, kv)


def attend_back_core(queries, keys, values, upstream, log_ref, bias_ref, store_q, store_kv, table):
    length = queries.shape[0]
    causal = bias_ref is not None
    masks = head_masks()
    step = length // 2
    key_grad = [None, None]
    value_grad = [None, None]

    def put(parts, at, term):
        parts[at] = term if parts[at] is None else parts[at] + term

    half = keys.shape[0] // 2
    for part in range(2):
        begin, end = part * step, (part + 1) * step
        reach = end if causal else keys.shape[0]
        query_grad = None
        for head in range(2):
            mask = masks[head]
            masked_keys = keys[:reach] * mask
            masked_query = queries[begin:end] * mask
            masked_up = upstream[begin:end] * mask
            scores = matmul_nt(masked_keys, queries[begin:end])
            if causal:
                scores = scores + bias_ref[head, :reach, begin:end].astype(F32)
            probs = jnp.exp(scores - log_ref[0, 0, head : head + 1, begin:end])
            prob_grad = matmul_nt(values[:reach], masked_up)
            delta = jnp.sum(probs * prob_grad, axis=0, keepdims=True)
            score_grad = probs * (prob_grad - delta)
            if table is not None:
                table(head, begin, end, reach, score_grad)
            low_grad = score_grad.astype(BF16)
            low_probs = probs.astype(BF16)
            for block in range(reach // half):
                rows = slice(block * half, (block + 1) * half)
                put(value_grad, block, matmul(low_probs[rows], masked_up))
                put(key_grad, block, matmul(low_grad[rows], masked_query))
            term = matmul_tn(masked_keys, low_grad)
            query_grad = term if query_grad is None else query_grad + term
        store_q(begin, end, jnp.transpose(query_grad).astype(BF16))
    for block in range(2):
        store_kv(
            block * half, (block + 1) * half, key_grad[block].astype(BF16), value_grad[block].astype(BF16)
        )


SHEAR = 128


def self_backward_kernel(qkv_ref, up_ref, log_ref, bias_ref, grad_ref, table_ref, shear_ref):
    length = qkv_ref.shape[0]

    @pl.when(pl.program_id(1) == 0)
    def _():
        shear_ref[...] = jnp.zeros_like(shear_ref)

    def table(head, begin, end, reach, score_grad):
        for block in range(reach // SHEAR):
            start = max(begin, block * SHEAR)
            shear_ref[head, :, start - block * SHEAR : end - block * SHEAR] += score_grad[
                block * SHEAR : (block + 1) * SHEAR, start - begin : end - begin
            ]

    def store_q(begin, end, grad):
        grad_ref[begin:end, :WIDE] = grad

    def store_kv(begin, end, key_grad, value_grad):
        grad_ref[begin:end, WIDE : 2 * WIDE] = key_grad
        grad_ref[begin:end, 2 * WIDE :] = value_grad

    attend_back_core(
        qkv_ref[:, :WIDE],
        qkv_ref[:, WIDE : 2 * WIDE],
        qkv_ref[:, 2 * WIDE :],
        up_ref[...],
        log_ref,
        bias_ref,
        store_q,
        store_kv,
        table,
    )

    @pl.when(pl.program_id(1) == pl.num_programs(1) - 1)
    def _():
        for head in range(2):
            total = shear_ref[head, 0:8, :]
            for group in range(1, SHEAR // 8):
                rows = shear_ref[head, 8 * group : 8 * group + 8, :]
                total = total + pltpu.roll(rows, length - 8 * group, 1)
            table_ref[head] = total


def cross_backward_kernel(q_ref, kv_ref, up_ref, log_ref, dq_ref, dkv_ref):
    def store_q(begin, end, grad):
        dq_ref[begin:end, :] = grad

    def store_kv(begin, end, key_grad, value_grad):
        dkv_ref[begin:end, :WIDE] = key_grad
        dkv_ref[begin:end, WIDE:] = value_grad

    attend_back_core(
        q_ref[...],
        kv_ref[:, :WIDE],
        kv_ref[:, WIDE:],
        up_ref[...],
        log_ref,
        None,
        store_q,
        store_kv,
        None,
    )


def self_backward(qkv, upstream, logs, bias, length):
    seqs = qkv.shape[0] // length
    return pl.pallas_call(
        self_backward_kernel,
        grid=(PAIRS, seqs),
        in_specs=[
            pl.BlockSpec((length, 3 * WIDE), lambda p, s: (s, p)),
            pl.BlockSpec((length, WIDE), lambda p, s: (s, p)),
            pl.BlockSpec((1, 1, 2, length), lambda p, s: (s, p, 0, 0)),
            pl.BlockSpec((2, length, length), lambda p, s: (p, 0, 0)),
        ],
        out_specs=[
            pl.BlockSpec((length, 3 * WIDE), lambda p, s: (s, p)),
            pl.BlockSpec((2, 8, length), lambda p, s: (p, 0, 0)),
        ],
        out_shape=[
            jax.ShapeDtypeStruct(qkv.shape, BF16),
            jax.ShapeDtypeStruct((HEADS, 8, length), F32),
        ],
        scratch_shapes=[pltpu.VMEM((2, SHEAR, length), F32)],
        compiler_params=params(),
        cost_estimate=pl.CostEstimate(
            flops=80_000_000_000, bytes_accessed=20_000_000, transcendentals=6_000_000
        ),
        name="self_backward",
    )(qkv, upstream, logs, bias)


def cross_backward(queries, kv, upstream, logs, length):
    seqs = queries.shape[0] // length
    extent = kv.shape[0] // seqs
    return pl.pallas_call(
        cross_backward_kernel,
        grid=(PAIRS, seqs),
        in_specs=[
            pl.BlockSpec((length, WIDE), lambda p, s: (s, p)),
            pl.BlockSpec((extent, 2 * WIDE), lambda p, s: (s, p)),
            pl.BlockSpec((length, WIDE), lambda p, s: (s, p)),
            pl.BlockSpec((1, 1, 2, length), lambda p, s: (s, p, 0, 0)),
        ],
        out_specs=[
            pl.BlockSpec((length, WIDE), lambda p, s: (s, p)),
            pl.BlockSpec((extent, 2 * WIDE), lambda p, s: (s, p)),
        ],
        out_shape=[
            jax.ShapeDtypeStruct(queries.shape, BF16),
            jax.ShapeDtypeStruct(kv.shape, BF16),
        ],
        compiler_params=params(),
        cost_estimate=pl.CostEstimate(
            flops=80_000_000_000, bytes_accessed=20_000_000, transcendentals=6_000_000
        ),
        name="cross_backward",
    )(queries, kv, upstream, logs)


DOWN_BLOCKS = -(-FF // D)
WIDTHS = (3 * INNER, D, INNER, 2 * INNER, D, 2 * FF, DOWN_BLOCKS * D)


def interleave(parts):
    rows = parts[0].shape[0]
    stacked = jnp.stack([part.reshape(rows, PAIRS, WIDE) for part in parts], axis=2)
    return stacked.reshape(rows, len(parts) * INNER)


def split_interleaved(block, count):
    rows = block.shape[0]
    stacked = block.reshape(rows, PAIRS, count, WIDE)
    return [stacked[:, :, at].reshape(-1) for at in range(count)]


def pack_shards(shards):
    rows = shards[0].shape[0] // D
    sq, sk, sv, so, cq, ck, cv, co = (shard.reshape(rows, D) for shard in shards[:8])
    gate, up = (shard.reshape(rows, FF) for shard in shards[8:10])
    down = shards[10].reshape(-1, D)
    down = jnp.pad(down, ((0, DOWN_BLOCKS * rows - down.shape[0]), (0, 0)))
    down = down.reshape(DOWN_BLOCKS, rows, D).transpose(1, 0, 2).reshape(rows, DOWN_BLOCKS * D)
    return jnp.concatenate(
        [interleave([sq, sk, sv]), so, cq, interleave([ck, cv]), co, gate, up, down], axis=1
    )


def unpack_down(block, count):
    rows = D // count
    stacked = block.reshape(count, rows, DOWN_BLOCKS, D).transpose(0, 2, 1, 3)
    stacked = stacked.reshape(count, DOWN_BLOCKS * rows, D)[:, : FF // count]
    return stacked.reshape(FF, D)


def pack_down(down, count):
    rows = D // count
    stacked = down.reshape(count, FF // count, D)
    stacked = jnp.pad(stacked, ((0, 0), (0, DOWN_BLOCKS * rows - FF // count), (0, 0)))
    stacked = stacked.reshape(count, DOWN_BLOCKS, rows, D).transpose(0, 2, 1, 3)
    return stacked.reshape(D, DOWN_BLOCKS * D)


def cut(block, widths):
    pieces = []
    start = 0
    for width in widths:
        pieces.append(block[:, start : start + width])
        start += width
    return pieces


def sum_everywhere(values, count):
    bit = 1
    while bit < count:
        pairs = [(index, index ^ bit) for index in range(count)]
        values = values + lax.ppermute(values, "fsdp", pairs)
        bit *= 2
    return values


def per_device(
    count,
    tokens,
    encoder_states,
    self_query,
    self_key,
    self_value,
    self_out,
    cross_query,
    cross_key,
    cross_value,
    cross_out,
    ff_gate,
    ff_up,
    ff_down,
    norm_gains,
    bias_table,
    buckets,
    cotangent,
):
    shards = (
        self_query,
        self_key,
        self_value,
        self_out,
        cross_query,
        cross_key,
        cross_value,
        cross_out,
        ff_gate,
        ff_up,
        ff_down,
    )
    gathered = lax.all_gather(pack_shards(shards), "fsdp", axis=0, tiled=True)
    w_qkv, w_so, w_cq, w_ckv, w_co, w_gu, w_down = cut(gathered, WIDTHS)
    w_down = unpack_down(w_down, count)

    gain_values = norm_gains.astype(F32)
    length = buckets.shape[0]
    bucket_of = buckets[:, 0]
    onehot = (bucket_of[None, :] == jnp.arange(BUCKETS, dtype=jnp.int32)[:, None]).astype(F32)
    distance_bias = jnp.take(bias_table, bucket_of, axis=0).T
    bias = expand_bias(distance_bias, length)

    inputs = tokens.astype(F32)
    factor_one = norm_factor(inputs)
    normed_one = (inputs * factor_one * gain_values[0]).astype(BF16)
    qkv = matmul(normed_one, w_qkv).astype(BF16)
    kv_two = matmul(encoder_states, w_ckv).astype(BF16)
    mixed_one, log_one = self_forward(qkv, bias, length)
    middle = inputs + matmul(mixed_one, w_so)
    factor_two = norm_factor(middle)
    normed_two = (middle * factor_two * gain_values[1]).astype(BF16)
    query_two = matmul(normed_two, w_cq).astype(BF16)
    mixed_two, log_two = cross_forward(query_two, kv_two, length)
    late = middle + matmul(mixed_two, w_co)
    factor_three = norm_factor(late)
    normed_three = (late * factor_three * gain_values[2]).astype(BF16)
    gate_rows = matmul(normed_three, w_gu[:, :FF])
    up_rows = matmul(normed_three, w_gu[:, FF:])
    activated, gelu_pull = jax.vjp(lambda gate: jax.nn.gelu(gate, approximate=True), gate_rows)
    hidden = (activated * up_rows).astype(BF16)
    result_rows = (late + matmul(hidden, w_down)).astype(BF16)

    grad_down = matmul_tn(hidden, cotangent).astype(BF16)
    hidden_grad = matmul_nt(cotangent, w_down)
    gate_grad = gelu_pull(hidden_grad * up_rows)[0].astype(BF16)
    up_grad = (hidden_grad * activated).astype(BF16)
    grad_gate = matmul_tn(normed_three, gate_grad).astype(BF16)
    grad_up = matmul_tn(normed_three, up_grad).astype(BF16)
    normed_grad = matmul_nt(gate_grad, w_gu[:, :FF]) + matmul_nt(up_grad, w_gu[:, FF:])
    norm_grad, gain_three = norm_backward(late, factor_three, gain_values[2], normed_grad)
    late_grad = cotangent.astype(F32) + norm_grad
    branch_grad = late_grad.astype(BF16)
    grad_co = matmul_tn(mixed_two, branch_grad).astype(BF16)
    mixed_grad = matmul_nt(branch_grad, w_co).astype(BF16)
    query_grad, kv_grad = cross_backward(query_two, kv_two, mixed_grad, log_two, length)
    grad_cq = matmul_tn(normed_two, query_grad).astype(BF16)
    grad_ckv = matmul_tn(encoder_states, kv_grad).astype(BF16)
    encoder_grad = matmul_nt(kv_grad, w_ckv).astype(BF16)
    norm_grad, gain_two = norm_backward(
        middle, factor_two, gain_values[1], matmul_nt(query_grad, w_cq)
    )
    middle_grad = late_grad + norm_grad
    branch_grad = middle_grad.astype(BF16)
    grad_so = matmul_tn(mixed_one, branch_grad).astype(BF16)
    mixed_grad = matmul_nt(branch_grad, w_so).astype(BF16)
    qkv_grad, sheared = self_backward(qkv, mixed_grad, log_one, bias, length)
    grad_qkv = matmul_tn(normed_one, qkv_grad).astype(BF16)
    norm_grad, gain_one = norm_backward(
        inputs, factor_one, gain_values[0], matmul_nt(qkv_grad, w_qkv)
    )
    input_grad = (middle_grad + norm_grad).astype(BF16)

    by_distance = sum(
        jnp.pad(sheared[:, row, row:], ((0, 0), (0, row))) for row in range(sheared.shape[1])
    )
    table_part = jnp.sum(onehot[:, None, :] * by_distance[None, :, :], axis=-1)

    packed = jnp.concatenate(
        [grad_qkv, grad_so, grad_cq, grad_ckv, grad_co, grad_gate, grad_up, pack_down(grad_down, count)],
        axis=1,
    )
    owned = lax.psum_scatter(packed, "fsdp", scatter_dimension=0, tiled=True).astype(F32)
    o_qkv, o_so, o_cq, o_ckv, o_co, o_gu, o_down = cut(owned, WIDTHS)
    g_sq, g_sk, g_sv = split_interleaved(o_qkv, 3)
    g_ck, g_cv = split_interleaved(o_ckv, 2)
    rows = owned.shape[0]
    g_down = o_down.reshape(rows, DOWN_BLOCKS, D).transpose(1, 0, 2).reshape(-1)[: FF // count * D]

    gains_part = jnp.stack([gain_one, gain_two, gain_three])
    small = jnp.concatenate([gains_part.reshape(-1), table_part.reshape(-1)]).reshape(-1, 128)
    small = sum_everywhere(small, count).reshape(-1)
    gains_grad = small[: 3 * D].reshape(3, D)
    table_grad = small[3 * D :].reshape(BUCKETS, HEADS)
    return (
        result_rows,
        input_grad,
        encoder_grad,
        g_sq,
        g_sk,
        g_sv,
        o_so.reshape(-1),
        o_cq.reshape(-1),
        g_ck,
        g_cv,
        o_co.reshape(-1),
        o_gu[:, :FF].reshape(-1),
        o_gu[:, FF:].reshape(-1),
        g_down,
        gains_grad,
        table_grad,
    )


def solution(mesh):
    flat = P("fsdp")
    rows = P("fsdp", None)
    return jax.shard_map(
        partial(per_device, mesh.shape["fsdp"]),
        mesh=mesh,
        in_specs=(rows, rows) + (flat,) * 11 + (P(), P(), P(), rows),
        out_specs=(rows, rows, rows) + (flat,) * 11 + (P(), P()),
        check_vma=False,
    )
```

time: 1540 us -> 612 us (0.40)
  waiting for transfers between devices: 874 us -> 278 us
  matrix products: 318 us -> 131 us
  local copies, waits for them, and re-layouts: 229 us -> 69.9 us
  Pallas kernels: 0 us -> 94.2 us
  blocking collectives: 40.4 us -> 0 us
  other arithmetic: 45.6 us -> 7.69 us
    unnamed x13 -> x2, waiting for transfers between devices: 441 us -> 0.03 us
    all_gather x11 -> x1, waiting for transfers between devices: 433 us -> 110 us  [per_device(): gathered = lax.all_gather(pack_shards(shards), 'fsdp', axis=0, tiled=True)]
    reduce_scatter x0 -> x1, waiting for transfers between devices: none -> 164 us  [per_device(): lax.psum_scatter(packed, 'fsdp', scatter_dimension=0, tiled=True)]
    dot_general x58 -> x8, matrix products: 210 us -> 60.3 us  [matmul(): return jnp.dot(left_side, right_side, preferred_element_type=F32)]
    pallas_call x0 -> x5, Pallas kernels: none -> 94.2 us  [the longest x1 28.1 us: cross_backward(): pl.pallas_call(cross_backward_kernel, grid=(PAIRS, seqs), in_specs=[pl.Bl...]
    convert_element_type x27 -> x0, local copies, waits for them, and re-layouts: 70.4 us -> none  [the longest x11 39.8 us: per_device(): one_grad.astype(jnp.bfloat16).astype(jnp.float32)]
    dynamic_slice x24 -> x0, local copies, waits for them, and re-layouts: 44.1 us -> none  [the longest x16 36.3 us: shrink_block(): grad_block = lax.dynamic_slice_in_dim(score_grad, start, block_rows, 2)]
    psum x1 -> x0, blocking collectives: 40.4 us -> none  [per_device(): gains_grad, table_grad = lax.psum((gains_sum, table_sum), 'fsdp')]
  transfers between devices with their start and end apart: 12 -> 7, of which waited for: 12 -> 4; matrix products, arithmetic and copies ran while one was open for 18% -> 8% of each run, Pallas kernels for 0% -> 1%
where the time goes in v1:
time: 612 us; the launch traced here: 602 us
  waiting for transfers between devices  278 us (45%)
  matrix products  131 us (21%)
  Pallas kernels  94.2 us (15%)
  local copies, waits for them, and re-layouts  69.9 us (11%)
  between operations  15.6 us (3%)
  other arithmetic  7.69 us (1%)
    reduce_scatter x1, waiting for transfers between devices, per_device(): lax.psum_scatter(packed, 'fsdp', scatter_dimension=0, tiled=True)  164 us
    all_gather x1, waiting for transfers between devices, per_device(): gathered = lax.all_gather(pack_shards(shards), 'fsdp', axis=0, tiled=True)  110 us
    dot_general x8, matrix products, matmul(): return jnp.dot(left_side, right_side, preferred_element_type=F32)  60.3 us
    dot_general x8, matrix products, matmul_nt(): lax.dot_general(left_side, right_side, (((1,), (1,)), ((), ())), preferre...  45.2 us
    pallas_call x1, Pallas kernels, cross_backward(): pl.pallas_call(cross_backward_kernel, grid=(PAIRS, seqs), in_specs=[pl.Bl...  28.1 us
    dot_general x8, matrix products, matmul_tn(): lax.dot_general(left_side, right_side, (((0,), (0,)), ((), ())), preferre...  25.6 us
    pallas_call x1, Pallas kernels, self_backward(): pl.pallas_call(self_backward_kernel, grid=(PAIRS, seqs), in_specs=[pl.Blo...  24.4 us
    unnamed x100, local copies, waits for them, and re-layouts  23.6 us
  transfers between devices with their start and end apart: 7, of which 4 were waited for; matrix products, arithmetic and copies ran while one was open for 8% of the time, Pallas kernels for 1%

profile of v1, /device:TPU:0, one launch (start us, length us, event | category | flops | bytes accessed | tf_op | source)
XLA Modules:
  0.0 601.5 jit_solution(2480203171744059508)
XLA Ops:
  10.7 1.4 reshape.190
  14.7 1.4 reshape.193
  25.1 1.6 copy.122
  26.9 1.7 slice_reduce_fusion
  34.9 5.9 bias.1.bias_ref
  40.8 2.7 copy.146
  43.9 110.5 %all-gather.2.cloned.1.call-done = bf16[768,12544]{1,0:T(8,128)(2,1)} async-done(((bf16[24,12544]{1,0:T(8,128)(2,1)}), bf16[768,12544]{1,0:T(8,128)(2,1)}) %all-gather.2.cloned.1.call-update) | async-done | bytes 19267600 | tf_op jit(solution)/shard_map/all_gather | solution.py:446
  154.4 7.8 %convolution_convert_fusion.qkv_ref = bf16[1024,2304]{1,0:T(8,128)(2,1)} fusion(bf16[768,12544]{1,0:T(8,128)(2,1)} %all-gather.2.cloned.1.call-done, bf16[1024,768]{0,1:T(8,128)(2,1)S(1)} %copy-done.7, f32[768]{0:T(1024)S(1)} %get-tuple-element.90, f32[1024]{0:T(1024)S(1)} %add_rsqrt_fusion.2), kind=kOutput, calls=%fused_computation.20 | convolution fusion | flops 3629383680 | bytes 9837568 | tf_op jit(solution)/shard_map/dot_general | solution.py:31
  162.2 17.0 %self_forward.1 = (bf16[1024,768]{1,0:T(8,128)(2,1)S(1)}, f32[2,6,2,512]{3,2,1,0:T(2,128)S(1)}) custom-call(bf16[1024,2304]{1,0:T(8,128)(2,1)} %convolution_convert_fusion.qkv_ref, bf16[12,512,512]{2,1,0:T(8,128)(2,1)} %bias.1.bias_ref), custom_call_target="tpu_custom_call" | custom-call | flops 40000000000 | bytes 16000000 | tf_op jit(solution)/shard_map/self_forward/pallas_call | solution.py:135
  179.2 3.4 multiply_reduce_fusion.5
  182.6 6.7 %fusion.13.kv_ref = bf16[1024,1536]{1,0:T(8,128)(2,1)} fusion(bf16[1024,768]{1,0:T(8,128)(2,1)S(1)} %copy-done, bf16[768,12544]{1,0:T(8,128)(2,1)} %all-gather.2.cloned.1.call-done), kind=kOutput, calls=%fused_computation.32 | convolution fusion | flops 2417491968 | bytes 7077888 | tf_op jit(solution)/shard_map/dot_general | solution.py:31
  189.3 2.8 convolution_convert_fusion.9.q_ref
  192.2 18.8 %cross_forward.1 = (bf16[1024,768]{1,0:T(8,128)(2,1)S(1)}, f32[2,6,2,512]{3,2,1,0:T(2,128)S(1)}) custom-call(bf16[1024,768]{1,0:T(8,128)(2,1)S(1)} %convolution_convert_fusion.9.q_ref, bf16[1024,1536]{1,0:T(8,128)(2,1)} %fusion.13.kv_ref), custom_call_target="tpu_custom_call" | custom-call | flops 40000000000 | bytes 16000000 | tf_op jit(solution)/shard_map/cross_forward/pallas_call | solution.py:161
  211.0 5.0 multiply_reduce_fusion.4
  216.0 4.0 slice.233
  220.0 8.8 %reshape.199 = bf16[32,24,3,768]{3,2,1,0:T(4,128)(2,1)} reshape(bf16[768,2304]{1,0:T(8,128)(2,1)} %slice.233) | data formatting | bytes 7077888 | tf_op jit(solution)/shard_map/reshape | solution.py:382
  228.8 2.9 copy.144
  233.3 5.7 fusion.75
  239.3 8.2 %fusion.31 = f32[1024,2048]{1,0:T(8,128)} fusion(bf16[1024,768]{0,1:T(8,128)(2,1)S(1)} %multiply_convert_fusion.1, bf16[768,12544]{1,0:T(8,128)(2,1)} %all-gather.2.cloned.1.call-done), kind=kOutput, calls=%fused_computation.61 | convolution fusion | flops 3221225472 | bytes 13107200 | tf_op jit(solution)/shard_map/dot_general | solution.py:31
  247.5 16.9 %fusion.6 = (bf16[1024,2048]{1,0:T(8,128)(2,1)S(1)}, bf16[1024,2048]{1,0:T(8,128)(2,1)}, bf16[1024,2048]{1,0:T(8,128)(2,1)}) fusion(f32[1024,2048]{1,0:T(8,128)} %fusion.31, f32[2048,1024]{0,1:T(8,128)} %fusion.75, bf16[1024,768]{0,1:T(8,128)(2,1)S(1)} %multiply_convert_fusion.1, bf16[768,12544]{1,0:T(8,128)(2,1)} %all-gather.2.cloned.1.call-done), kind=kOutput, calls=%fused_computation.9 | convolution fusion | flops 3275751424 | bytes 34078720 | tf_op jit(solution)/shard_map/dot_general | solution.py:31
  264.4 7.7 %fusion.29 = f32[1024,768]{0,1:T(8,128)S(1)} fusion(bf16[1024,2048]{1,0:T(8,128)(2,1)} %get-tuple-element.92, bf16[768,12544]{1,0:T(8,128)(2,1)} %all-gather.2.cloned.1.call-done), kind=kOutput, calls=%fused_computation.59 | convolution fusion | flops 3221225472 | bytes 10485760 | tf_op jit(solution)/shard_map/dot_general | solution.py:41
  272.1 6.6 %multiply_reduce_fusion = (f32[768]{0:T(1024)}, f32[1024]{0:T(1024)S(1)}, f32[1024,768]{0,1:T(8,128)S(1)}) fusion(f32[1024,768]{0,1:T(8,128)S(1)} %copy-done.5, f32[1024]{0:T(1024)S(1)} %add_rsqrt_fusion, f32[768]{0:T(1024)S(1)} %get-tuple-element.88, f32[1024,768]{0,1:T(8,128)S(1)} %fusion.29, bf16[1024,2048]{1,0:T(8,128)(2,1)S(1)} %get-tuple-element.91, ...), kind=kOutput, calls=%fused_computation.43 | convolution fusion | flops 3226728704 | bytes 16791552 | tf_op jit(solution)/shard_map/dot_general | solution.py:41
  279.6 2.7 convolution_convert_fusion.8.up_ref
  282.4 28.1 %cross_backward.1 = (bf16[1024,768]{1,0:T(8,128)(2,1)S(1)}, bf16[1024,1536]{1,0:T(8,128)(2,1)}) custom-call(bf16[1024,768]{1,0:T(8,128)(2,1)S(1)} %convolution_convert_fusion.9.q_ref, bf16[1024,1536]{1,0:T(8,128)(2,1)} %fusion.13.kv_ref, bf16[1024,768]{1,0:T(8,128)(2,1)S(1)} %convolution_convert_fusion.8.up_ref, f32[2,6,2,512]{3,2,1,0:T(2,128)S(1)} %get-tuple-element.26.log_ref), custom_call_target="tpu_custom_call" | custom-call | flops 80000000000 | bytes 20000000 | tf_op jit(solution)/shard_map/cross_backward/pallas_call | solution.py:327
  310.5 3.0 multiply_reduce_fusion.1
  314.3 3.6 convolution_convert_fusion.7.up_ref
  317.9 24.4 %self_backward.1 = (bf16[1024,2304]{1,0:T(8,128)(2,1)}, f32[12,8,512]{2,1,0:T(8,128)S(1)}) custom-call(bf16[1024,2304]{1,0:T(8,128)(2,1)} %convolution_convert_fusion.qkv_ref, bf16[1024,768]{1,0:T(8,128)(2,1)S(1)} %convolution_convert_fusion.7.up_ref, f32[2,6,2,512]{3,2,1,0:T(2,128)S(1)} %get-tuple-element.28.log_ref, bf16[12,512,512]{2,1,0:T(8,128)(2,1)} %bias.1.bias_ref), custom_call_target="tpu_custom_call" | custom-call | flops 80000000000 | bytes 20000000 | tf_op jit(solution)/shard_map/self_backward/pallas_call | solution.py:298
  342.4 6.7 %fusion.8 = bf16[768,12544]{1,0:T(8,128)(2,1)S(1)} fusion(bf16[1024,2304]{1,0:T(8,128)(2,1)} %get-tuple-element.29, bf16[1024,768]{0,1:T(8,128)(2,1)S(1)} %copy-done.8, f32[768]{0:T(1024)S(1)} %copy-done.28, f32[1024]{0:T(1024)S(1)} %copy-done.24), kind=kOutput, calls=%fused_computation.22 | convolution fusion | flops 3628793856 | bytes 9837568 | tf_op jit(solution)/shard_map/dot_general | solution.py:35
  349.1 1.4 fusion.48
  350.6 1.4 fusion.47
  352.4 3.1 fusion.28
  355.6 1.5 fusion.46
  358.2 3.7 fusion.12
  361.9 3.7 fusion.11
  365.7 4.1 convolution_convert_fusion.4
  369.7 2.4 copy-done.6
  372.4 2.3 copy.156
  375.5 2.1 constant_dynamic-update-slice_fusion.8
  379.4 9.6 %fusion.23 = (f32[768]{0:T(1024)S(1)}, f32[1024]{0:T(1024)S(1)}, f32[1024,768]{0,1:T(8,128)}) fusion(bf16[1024,768]{0,1:T(8,128)(2,1)S(1)} %copy-done.8, f32[1024]{0:T(1024)S(1)} %copy-done.24, f32[768]{0:T(1024)S(1)} %copy-done.28, bf16[1024,2304]{1,0:T(8,128)(2,1)} %get-tuple-element.29, bf16[768,12544]{1,0:T(8,128)(2,1)} %all-gather.2.cloned.1.call-done), kind=kOutput, calls=%fused_computation.42 | convolution fusion | flops 3629381888 | bytes 12990464 | tf_op jit(solution)/shard_map/dot_general | solution.py:41
  390.3 1.5 collective-permute-start.1
  391.7 9.5 %add_convert_fusion = bf16[1024,768]{0,1:T(8,128)(2,1)} fusion(f32[1024,768]{0,1:T(8,128)} %get-tuple-element.109, bf16[1024,2048]{1,0:T(8,128)(2,1)} %get-tuple-element.93, bf16[2048,768]{1,0:T(8,128)(2,1)} %bitcast.142), kind=kOutput, calls=%fused_computation.49 | convolution fusion | flops 3222798336 | bytes 12058624 | tf_op jit(solution)/shard_map/dot_general | solution.py:31
  402.0 6.3 %fusion.43 = bf16[1024,768]{1,0:T(8,128)(2,1)} fusion(bf16[1024,1536]{1,0:T(8,128)(2,1)S(1)} %copy-done.38, bf16[768,12544]{1,0:T(8,128)(2,1)} %all-gather.2.cloned.1.call-done), kind=kOutput, calls=%fused_computation.72 | convolution fusion | flops 2416705536 | bytes 7077888 | tf_op jit(solution)/shard_map/dot_general | solution.py:41
  408.9 3.2 collective-permute-done.3
  412.1 1.7 collective-permute-start.4
  413.7 2.1 fusion.19
  415.8 2.8 copy.168
  418.6 1.6 copy.169
  421.6 163.7 %reduce-scatter.2.cloned.1.call-done = bf16[24,12544]{1,0:T(8,128)(2,1)} async-done(((bf16[768,12544]{1,0:T(8,128)(2,1)}), bf16[24,12544]{1,0:T(8,128)(2,1)}) %reduce-scatter.2.cloned.1.call-update) | async-done | bytes 602128 | tf_op jit(solution)/shard_map/reduce_scatter | solution.py:516
  (233 shorter events, 42.4 us)
Async XLA Ops:
  7.2 175.4 %copy-start = (bf16[1024,768]{1,0:T(8,128)(2,1)S(1)}, bf16[1024,768]{1,0:T(8,128)(2,1)}, u32[]{:S(2)}) copy-start(bf16[1024,768]{1,0:T(8,128)(2,1)} %param.18) | copy-start | bytes 4718596
  7.2 17.9 %copy-start.18 = (bf16[1024,768]{1,0:T(8,128)(2,1)S(1)}, bf16[1024,768]{1,0:T(8,128)(2,1)}, u32[]{:S(2)}) copy-start(bf16[1024,768]{1,0:T(8,128)(2,1)} %param.17) | copy-start | bytes 4718596
  7.2 147.2 %all-gather.2.cloned.1.call-start = ((), (), s32[]{:S(2)}) async-start(), calls=%async_computation.1 | async-start | bytes 19869696 | tf_op jit(solution)/shard_map/all_gather | solution.py:446
  14.5 12.2 %copy-start.33 = (bf16[32,12]{0,1:T(8,128)(2,1)S(1)}, bf16[32,12]{0,1:T(8,128)(2,1)}, u32[]{:S(2)}) copy-start(bf16[32,12]{0,1:T(8,128)(2,1)} %param.31) | copy-start | bytes 2308
  19.0 7.7 %copy-start.32 = (bf16[3,768]{1,0:T(4,128)(2,1)S(1)}, bf16[3,768]{1,0:T(4,128)(2,1)}, u32[]{:S(2)}) copy-start(bf16[3,768]{1,0:T(4,128)(2,1)} %param.30) | copy-start | bytes 13828
  25.1 560.2 %reduce-scatter.2.cloned.1.call-start = ((), (), s32[]{:S(2)}) async-start(), calls=%async_computation.2 | async-start | bytes 19869696 | tf_op jit(solution)/shard_map/reduce_scatter | solution.py:516
  40.8 2.7 copy-start.7
  43.5 110.9 %copy-start.27 = (f32[768]{0:T(1024)}, f32[768]{0:T(1024)S(1)}, u32[]{:S(2)}) copy-start(f32[768]{0:T(1024)S(1)} %get-tuple-element.90) | copy-start | bytes 9220
  43.5 145.8 %copy-start.29 = (f32[768]{0:T(1024)}, f32[768]{0:T(1024)S(1)}, u32[]{:S(2)}) copy-start(f32[768]{0:T(1024)S(1)} %get-tuple-element.89) | copy-start | bytes 9220
  43.9 110.5 %copy-start.23 = (f32[1024]{0:T(1024)}, f32[1024]{0:T(1024)S(1)}, u32[]{:S(2)}) copy-start(f32[1024]{0:T(1024)S(1)} %add_rsqrt_fusion.2) | copy-start | bytes 12292
  179.2 3.4 copy-start.3
  182.6 28.4 %copy-start.11 = (f32[1024,768]{0,1:T(8,128)}, f32[1024,768]{0,1:T(8,128)S(1)}, u32[]{:S(2)}) copy-start(f32[1024,768]{0,1:T(8,128)S(1)} %get-tuple-element.107) | copy-start | bytes 9437188
  182.6 6.7 %copy-start.25 = (f32[1024]{0:T(1024)}, f32[1024]{0:T(1024)S(1)}, u32[]{:S(2)}) copy-start(f32[1024]{0:T(1024)S(1)} %add_rsqrt_fusion.1) | copy-start | bytes 12292
  211.0 5.0 copy-start.1
  231.7 1.6 copy-start.19
  232.1 6.8 %copy-start.17 = (bf16[32,64,768]{2,1,0:T(8,128)(2,1)}, bf16[32,64,768]{2,1,0:T(8,128)(2,1)S(1)}, u32[]{:S(2)}) copy-start(bf16[32,64,768]{2,1,0:T(8,128)(2,1)S(1)} %slice.234) | copy-start | bytes 9437188
  233.3 5.7 copy-start.5
  239.3 8.2 %copy-start.21 = (bf16[1024,768]{0,1:T(8,128)(2,1)}, bf16[1024,768]{0,1:T(8,128)(2,1)S(1)}, u32[]{:S(2)}) copy-start(bf16[1024,768]{0,1:T(8,128)(2,1)S(1)} %multiply_convert_fusion.1) | copy-start | bytes 4718596
  264.4 7.7 %copy-start.35 = (bf16[1024,2048]{1,0:T(8,128)(2,1)}, bf16[1024,2048]{1,0:T(8,128)(2,1)S(1)}, u32[]{:S(2)}) copy-start(bf16[1024,2048]{1,0:T(8,128)(2,1)S(1)} %get-tuple-element.91) | copy-start | bytes 12582916
  272.1 6.7 %copy-start.14 = (bf16[1024,768]{0,1:T(8,128)(2,1)S(1)}, bf16[1024,768]{0,1:T(8,128)(2,1)}, u32[]{:S(2)}) copy-start(bf16[1024,768]{0,1:T(8,128)(2,1)} %copy.146) | copy-start | bytes 4718596
  282.4 28.1 %copy-start.12 = (f32[1024,768]{0,1:T(8,128)S(1)}, f32[1024,768]{0,1:T(8,128)}, u32[]{:S(2)}) copy-start(f32[1024,768]{0,1:T(8,128)} %copy-done.11) | copy-start | bytes 9437188
  282.4 28.1 %copy-start.26 = (f32[1024]{0:T(1024)S(1)}, f32[1024]{0:T(1024)}, u32[]{:S(2)}) copy-start(f32[1024]{0:T(1024)} %copy-done.25) | copy-start | bytes 12292
  282.4 28.1 %copy-start.30 = (f32[768]{0:T(1024)S(1)}, f32[768]{0:T(1024)}, u32[]{:S(2)}) copy-start(f32[768]{0:T(1024)} %copy-done.29) | copy-start | bytes 9220
  314.2 34.8 %copy-start.9 = (f32[1024,768]{0,1:T(8,128)}, f32[1024,768]{0,1:T(8,128)S(1)}, u32[]{:S(2)}) copy-start(f32[1024,768]{0,1:T(8,128)S(1)} %multiply_add_fusion) | copy-start | bytes 9437188
  317.9 24.5 %copy-start.8 = (bf16[1024,768]{0,1:T(8,128)(2,1)S(1)}, bf16[1024,768]{0,1:T(8,128)(2,1)}, u32[]{:S(2)}) copy-start(bf16[1024,768]{0,1:T(8,128)(2,1)} %copy.122) | copy-start | bytes 4718596
  317.9 24.5 %copy-start.24 = (f32[1024]{0:T(1024)S(1)}, f32[1024]{0:T(1024)}, u32[]{:S(2)}) copy-start(f32[1024]{0:T(1024)} %copy-done.23) | copy-start | bytes 12292
  317.9 24.5 %copy-start.28 = (f32[768]{0:T(1024)S(1)}, f32[768]{0:T(1024)}, u32[]{:S(2)}) copy-start(f32[768]{0:T(1024)} %copy-done.27) | copy-start | bytes 9220
  342.4 6.7 %copy-start.4 = (bf16[1024,768]{1,0:T(8,128)(2,1)S(1)}, bf16[1024,768]{1,0:T(8,128)(2,1)}, u32[]{:S(2)}) copy-start(bf16[1024,768]{1,0:T(8,128)(2,1)} %copy-done.3) | copy-start | bytes 4718596
  350.5 1.9 copy-start.37
  352.4 3.1 copy-start.2
  355.6 1.5 copy-start.22
  355.6 2.7 copy-start.36
  358.2 3.7 copy-start.39
  361.9 3.7 copy-start.20
  361.9 3.7 copy-start.40
  365.6 6.5 %copy-start.6 = (bf16[768,12544]{1,0:T(8,128)(2,1)}, bf16[768,12544]{1,0:T(8,128)(2,1)S(1)}, u32[]{:S(2)}) copy-start(bf16[768,12544]{1,0:T(8,128)(2,1)S(1)} %fusion.11) | copy-start | bytes 57802756
  377.6 0.7 copy-start.31
  377.6 1.8 copy-start.34
  389.0 1.2 collective-permute-start
  390.3 11.8 %copy-start.38 = (bf16[1024,1536]{1,0:T(8,128)(2,1)S(1)}, bf16[1024,1536]{1,0:T(8,128)(2,1)}, u32[]{:S(2)}) copy-start(bf16[1024,1536]{1,0:T(8,128)(2,1)} %get-tuple-element.30) | copy-start | bytes 9437188
  390.3 10.9 %collective-permute-start.1 = (f32[21,128]{1,0:T(8,128)S(1)}, f32[21,128]{1,0:T(8,128)S(1)}, u32[]{:S(2)}, u32[]{:S(2)}) collective-permute-start(f32[21,128]{1,0:T(8,128)S(1)} %fusion.102), channel_id=1, source_target_pairs={{0,2},{1,3},{2,0},{3,1},{4,6},{5,7},{6,4},{7,5},{8,10},{9,11},{10,... | collective-permute-start | bytes 32264 | tf_op jit(solution)/shard_map/ppermute | solution.py:408
  401.2 12.5 %copy-start.10 = (f32[1024,768]{0,1:T(8,128)S(1)}, f32[1024,768]{0,1:T(8,128)}, u32[]{:S(2)}) copy-start(f32[1024,768]{0,1:T(8,128)} %copy-done.9) | copy-start | bytes 9437188
  401.2 12.5 %copy-start.16 = (f32[1024,768]{0,1:T(8,128)S(1)}, f32[1024,768]{0,1:T(8,128)}, u32[]{:S(2)}) copy-start(f32[1024,768]{0,1:T(8,128)} %get-tuple-element.112) | copy-start | bytes 9437188
  401.2 7.1 %collective-permute-start.2 = (f32[21,128]{1,0:T(8,128)S(1)}, f32[21,128]{1,0:T(8,128)S(1)}, u32[]{:S(2)}, u32[]{:S(2)}) collective-permute-start(f32[21,128]{1,0:T(8,128)S(1)} %fusion.103), channel_id=1, source_target_pairs={{0,4},{1,5},{2,6},{3,7},{4,0},{5,1},{6,2},{7,3},{8,12},{9,13},{10,... | collective-permute-start | bytes 32264 | tf_op jit(solution)/shard_map/ppermute | solution.py:408
  408.3 3.8 collective-permute-start.3
  412.1 8.1 %collective-permute-start.4 = (f32[21,128]{1,0:T(8,128)S(1)}, f32[21,128]{1,0:T(8,128)S(1)}, u32[]{:S(2)}, u32[]{:S(2)}) collective-permute-start(f32[21,128]{1,0:T(8,128)S(1)} %add.174), channel_id=1, source_target_pairs={{0,16},{1,17},{2,18},{3,19},{4,20},{5,21},{6,22},{7,23},{8,24},{9,... | collective-permute-start | bytes 32264 | tf_op jit(solution)/shard_map/ppermute | solution.py:408
  415.8 2.8 copy-start.13
  585.3 6.5 %copy-start.15 = (bf16[24,12544]{1,0:T(8,128)(2,1)S(1)}, bf16[24,12544]{1,0:T(8,128)(2,1)}, u32[]{:S(2)}) copy-start(bf16[24,12544]{1,0:T(8,128)(2,1)} %reduce-scatter.2.cloned.1.call-done) | copy-start | bytes 1806340
Sparse Core Ops, SparseCore 0:
  25.2 129.1 all-gather.1
  377.7 207.5 reduce-scatter.1
